TPU v7x, 32 devices: a whole 2x2x4 slice. The times are simulated.
32 devices in a mesh: groups: 2 (over y), pairs: 8 (over z, x), rows: 2 (over core).
Axes of the slice: x: 2, y: 2, z: 4, core: 2. Of those that a mesh axis runs over, the one named last changes fastest.
Arguments:
- images: bfloat16 [128, 16, 768], P('groups', ('pairs', 'rows')), parts along dimension 0, may hold values from -12 to 12
- w_qkv: bfloat16 [768, 2304], replicated, may hold values from -0.21875 to 0.21875
- w_out: bfloat16 [768, 768], replicated, may hold values from -0.21875 to 0.21875
- pair_list: int32 [48, 2], P('groups'), parts along dimension 0, may hold values from 0 to 63, as said below
- pair_weight: int32 [48], P('groups'), parts along dimension 0, may hold values from 0 to 4, as said below
Outputs:
- mixed: bfloat16 [128, 16, 768], P('groups', ('pairs', 'rows')), parts along dimension 0
There are 2 independent parts, one for each index of `groups`. A program takes and returns all parts, laid end to end along the dimension named above; an argument that names none is the same for every part. Nothing has to cross between parts.
Inputs may be any that keep to these rules, and one draw needn't show every extreme that they name: `pair_list`: the two images of a slot differ. `pair_weight`: A slot is live when its weight is positive. Slots 3 * g to 3 * g + 2 form pair group g, and group g belongs to device g along pairs. Exactly 16 slots are live, and in every draw some group has all 3 slots live.
All inputs are finite; a program needn't handle non-finite values.
Results may differ from a plain program's by a relative error of at most 0.0034.
Values may be sent and summed in bfloat16 or wider, within the bound.
A program may use at most 64 MiB of HBM per device.

v0:
```python
import jax
import jax.numpy as jnp
from jax import lax
from jax.sharding import PartitionSpec as P

D = 768
HEADS = 12
HDIM = 64
IMGS = 64
PMAX = 3


def cross_both(queries, key_rows, value_rows):
    item_count = queries.shape[0]
    query_len = queries.shape[2]
    key_len = key_rows.shape[2]
    batch = item_count * 2
    split_q = queries.reshape(batch, query_len, HEADS, HDIM)
    split_k = key_rows[:, ::-1].reshape(batch, key_len, HEADS, HDIM)
    split_v = value_rows[:, ::-1].reshape(batch, key_len, HEADS, HDIM)
    scores = jnp.einsum(
        "nqhc,nshc->nhqs", split_q, split_k, preferred_element_type=jnp.float32
    ) * HDIM ** (-0.5)
    largest = jnp.max(scores, axis=3, keepdims=True)
    exponent = jnp.exp(scores - largest)
    softmax = (exponent / jnp.sum(exponent, axis=3, keepdims=True)).astype(jnp.bfloat16)
    blended = jnp.einsum("nhqs,nshc->nqhc", softmax, split_v, preferred_element_type=jnp.float32)
    return blended.reshape(1, item_count, 2, query_len, D)


def local(images, w_qkv, w_out, pair_list, pair_weight):
    devices = lax.axis_size("pairs")
    device = lax.axis_index("pairs")
    local_tokens = images.shape[1]
    table_ends = pair_list.reshape(devices, PMAX, 2)
    slot_weight = pair_weight.reshape(devices, PMAX)
    my_weight = lax.dynamic_index_in_dim(slot_weight, device, 0, keepdims=False).astype(jnp.float32)
    flat_images = images.reshape(IMGS * local_tokens, D)
    projected = jnp.dot(flat_images, w_qkv, preferred_element_type=jnp.float32)
    projected = projected.astype(jnp.bfloat16).reshape(IMGS, local_tokens, 3 * D)
    outgoing = projected[table_ends]
    own_half = lax.all_to_all(outgoing, "pairs", split_axis=0, concat_axis=3, tiled=True)[0]
    gathered = lax.all_gather(own_half[..., D:], "rows", axis=2, tiled=True)
    attended = cross_both(own_half[..., :D], gathered[..., :D], gathered[..., D:])
    message = (attended * my_weight[None, :, None, None, None]).astype(jnp.bfloat16)
    returned = lax.all_to_all(message, "pairs", split_axis=3, concat_axis=0, tiled=True)
    item_count = returned.shape[1]
    flat_back = returned.reshape(devices * item_count * 2, local_tokens * D)
    selector = (
        table_ends.reshape(-1)[:, None] == jnp.arange(IMGS, dtype=jnp.int32)[None, :]
    ).astype(jnp.bfloat16)
    summed = lax.dot_general(
        selector, flat_back, (((0,), (0,)), ((), ())), preferred_element_type=jnp.float32
    )
    matches = (pair_list[None, :, :] == jnp.arange(IMGS, dtype=jnp.int32)[:, None, None]).astype(
        jnp.float32
    )
    totals = 1.0 + jnp.sum(matches * pair_weight.astype(jnp.float32)[None, :, None], axis=(1, 2))
    average = (summed / totals[:, None]).astype(jnp.bfloat16)
    update = jnp.dot(average, w_out, preferred_element_type=jnp.float32)
    result = flat_images.astype(jnp.float32) + update
    return result.astype(jnp.bfloat16).reshape(images.shape)


def solution(mesh):
    in_specs = (P("groups", ("pairs", "rows"), None), P(), P(), P("groups", None), P("groups"))
    out_specs = P("groups", ("pairs", "rows"), None)
    return jax.shard_map(local, mesh=mesh, in_specs=in_specs, out_specs=out_specs, check_vma=False)
```

profile of v0, /device:TPU:0, one launch (start us, length us, event | category | flops | bytes accessed | tf_op | source)
XLA Modules:
  0.0 70.6 jit_solution(13591852283024392134)
XLA Ops:
  3.6 2.3 %convolution_convert_fusion = bf16[64,2304]{1,0:T(8,128)(2,1)} fusion(bf16[768,2304]{1,0:T(8,128)(2,1)S(1)} %copy-done, bf16[64,1,768]{2,0,1:T(8,128)(2,1)} %param.5), kind=kOutput, calls=%fused_computation.2 | convolution fusion | flops 226639872 | bytes 3932160 | tf_op jit(solution)/shard_map/dot_general | solution.py:39
  6.0 2.6 %gather_fusion = bf16[48,2304]{1,0:T(8,128)(2,1)} fusion(bf16[64,2304]{1,0:T(8,128)(2,1)} %convolution_convert_fusion, s32[1024]{0:T(1024)S(1)} %pad_clamp_fusion), kind=kCustom, calls=%fused_computation | custom fusion | bytes 442560 | tf_op jit(solution)/shard_map/gather | solution.py:41
  8.6 1.7 %reshape.103 = bf16[8,3,2,1,2304]{4,2,1,0,3:T(2,128)(2,1)} reshape(bf16[48,2304]{1,0:T(8,128)(2,1)} %gather_fusion) | data formatting | bytes 442368 | tf_op jit(solution)/shard_map/gather | solution.py:41
  10.3 7.3 %all-to-all-start = ((bf16[8,3,2,1,2304]{4,2,1,3,0:T(2,128)(2,1)}), bf16[8,3,2,1,2304]{4,2,1,3,0:T(2,128)(2,1)}, u32[]{:S(2)}, u32[]{:S(2)}) async-start(bf16[8,3,2,1,2304]{4,2,1,3,0:T(2,128)(2,1)} %bitcast.36), calls=%async_computation | async-start | bytes 442368 | tf_op jit(solution)/shard_map/all_to_all | solution.py:42
  17.6 1.3 %reshape.99 = s32[8,3]{1,0:T(8,128)} reshape(s32[24]{0:T(128)} %param.9) | data formatting | bytes 192 | tf_op jit(solution)/shard_map/reshape | solution.py:36
  19.0 1.2 %convert_element_type.47 = f32[24]{0:T(128)} convert(s32[24]{0:T(128)} %param.9) | non-fusion elementwise | flops 24 | bytes 192 | tf_op jit(solution)/shard_map/convert_element_type | solution.py:58
  22.3 3.7 %all-to-all-done = bf16[8,3,2,1,2304]{4,2,1,3,0:T(2,128)(2,1)} async-done(((bf16[8,3,2,1,2304]{4,2,1,3,0:T(2,128)(2,1)}), bf16[8,3,2,1,2304]{4,2,1,3,0:T(2,128)(2,1)}, u32[]{:S(2)}, u32[]{:S(2)}) %all-to-all-start) | async-done | bytes 221216 | tf_op jit(solution)/shard_map/all_to_all | solution.py:42
  26.0 1.0 %slice.18 = bf16[3,2,8,1536]{3,1,0,2:T(2,128)(2,1)S(1)} slice(bf16[3,2,8,2304]{3,1,0,2:T(2,128)(2,1)} %bitcast.4), slice={[0:3], [0:2], [0:8], [768:2304]} | slice | bytes 294912 | tf_op jit(solution)/shard_map/slice | solution.py:43
  27.0 1.6 %slice.20 = bf16[3,2,8,768]{3,1,0,2:T(2,128)(2,1)} slice(bf16[3,2,8,2304]{3,1,0,2:T(2,128)(2,1)} %bitcast.4), slice={[0:3], [0:2], [0:8], [0:768]} | slice | bytes 147456 | tf_op jit(solution)/shard_map/slice | solution.py:44
  28.5 2.0 %all_gather.3 = bf16[3,2,16,1536]{3,1,0,2:T(2,128)(2,1)S(1)} all-gather(bf16[3,2,8,1536]{3,1,0,2:T(2,128)(2,1)S(1)} %slice.18), channel_id=1, replica_groups=mesh['groups'=2,'pairs'=8,'rows'=2] {'rows'}, dimensions={2}, use_global_device_ids=true | all-gather | bytes 442368 | tf_op jit(solution)/shard_map/all_gather | solution.py:43
  31.5 3.7 %rev.7 = bf16[3,2,16,768]{3,1,0,2:T(2,128)(2,1)} reverse(bf16[3,2,16,768]{3,1,0,2:T(2,128)(2,1)} %get-tuple-element.5), dimensions={1} | reverse | bytes 294912 | tf_op jit(solution)/shard_map/rev | solution.py:19
  35.2 1.9 %reshape.117 = bf16[6,16,12,64]{3,2,0,1:T(8,128)(2,1)} reshape(bf16[3,2,16,768]{3,1,0,2:T(2,128)(2,1)} %rev.7) | data formatting | bytes 294912 | tf_op jit(solution)/shard_map/reshape | solution.py:19
  37.1 1.7 %reshape.116 = bf16[6,8,12,64]{3,2,0,1:T(8,128)(2,1)} reshape(bf16[3,2,8,768]{3,1,0,2:T(2,128)(2,1)} %slice.20) | data formatting | bytes 147456 | tf_op jit(solution)/shard_map/reshape | solution.py:18
  38.8 1.4 %convolution_multiply_fusion = f32[6,12,8,16]{3,2,1,0:T(8,128)S(1)} fusion(bf16[6,16,12,64]{3,2,0,1:T(8,128)(2,1)} %reshape.117, bf16[6,8,12,64]{3,2,0,1:T(8,128)(2,1)} %reshape.116), kind=kOutput, calls=%fused_computation.5 | convolution fusion | flops 1188864 | bytes 258048 | tf_op jit(solution)/shard_map/nqhc,nshc->nhqs/dot_general | solution.py:21
  41.8 3.7 %rev.6 = bf16[3,2,16,768]{3,1,0,2:T(2,128)(2,1)} reverse(bf16[3,2,16,768]{3,1,0,2:T(2,128)(2,1)} %get-tuple-element.6), dimensions={1} | reverse | bytes 294912 | tf_op jit(solution)/shard_map/rev | solution.py:20
  45.5 1.9 %reshape.115 = bf16[6,16,12,64]{3,2,0,1:T(8,128)(2,1)} reshape(bf16[3,2,16,768]{3,1,0,2:T(2,128)(2,1)} %rev.6) | data formatting | bytes 294912 | tf_op jit(solution)/shard_map/reshape | solution.py:20
  47.4 3.0 %convolution_bitcast_fusion = f32[6,8,12,64]{3,1,2,0:T(8,128)} fusion(bf16[6,16,12,64]{3,2,0,1:T(8,128)(2,1)} %reshape.115, f32[6,12,8]{2,1,0:T(8,128)} %fusion.15, f32[6,12,8,16]{3,2,1,0:T(8,128)} %copy-done.1), kind=kOutput, calls=%fused_computation.4 | convolution fusion | flops 1207887 | bytes 334080 | tf_op jit(solution)/shard_map/nhqs,nshc->nqhc/dot_general | solution.py:27
  50.4 1.8 %copy.51 = f32[6,8,12,64]{3,2,1,0:T(8,128)} copy(f32[6,8,12,64]{3,1,2,0:T(8,128)} %convolution_bitcast_fusion) | data formatting | bytes 294912 | tf_op jit(solution)/shard_map/nhqs,nshc->nqhc/transpose | solution.py:27
  52.2 1.8 %reshape.98 = f32[1,3,2,8,768]{4,3,2,1,0:T(8,128)} reshape(f32[6,8,12,64]{3,2,1,0:T(8,128)} %copy.51) | data formatting | bytes 294912 | tf_op jit(solution)/shard_map/reshape | solution.py:28
  53.9 1.0 %multiply_convert_fusion = bf16[1,3,2,8,768]{4,3,2,1,0:T(8,128)(2,1)S(1)} fusion(f32[1,3,2,8,768]{4,3,2,1,0:T(8,128)} %reshape.98, f32[3]{0:T(128)S(1)} %convert_bitcast_fusion), kind=kLoop, calls=%fused_computation.16 | loop fusion | flops 73728 | bytes 221196 | tf_op jit(solution)/shard_map/convert_element_type | solution.py:45
  55.6 4.0 %all-to-all-start.1 = ((bf16[1,3,2,8,768]{4,2,1,0,3:T(2,128)(2,1)}), bf16[1,3,2,8,768]{4,2,1,0,3:T(2,128)(2,1)}, u32[]{:S(2)}, u32[]{:S(2)}) async-start(bf16[1,3,2,8,768]{4,2,1,0,3:T(2,128)(2,1)} %copy.52), calls=%async_computation.1 | async-start | bytes 147456 | tf_op jit(solution)/shard_map/all_to_all | solution.py:46
  59.6 7.0 %all-to-all-done.1 = bf16[1,3,2,8,768]{4,2,1,0,3:T(2,128)(2,1)} async-done(((bf16[1,3,2,8,768]{4,2,1,0,3:T(2,128)(2,1)}), bf16[1,3,2,8,768]{4,2,1,0,3:T(2,128)(2,1)}, u32[]{:S(2)}, u32[]{:S(2)}) %all-to-all-start.1) | async-done | bytes 73760 | tf_op jit(solution)/shard_map/all_to_all | solution.py:46
  66.6 1.5 %reshape.100 = bf16[48,768]{1,0:T(8,128)(2,1)} reshape(bf16[8,1,3,2,1,768]{5,3,2,0,4,1:T(2,128)(2,1)} %bitcast.10) | data formatting | bytes 147456 | tf_op jit(solution)/shard_map/reshape | solution.py:48
  68.1 2.5 %fusion.5 = bf16[64,1,768]{2,0,1:T(8,128)(2,1)} fusion(bf16[768,768]{1,0:T(8,128)(2,1)} %param.7, bf16[48,768]{1,0:T(8,128)(2,1)} %reshape.100, bf16[64,1,768]{2,0,1:T(8,128)(2,1)} %param.5, f32[64]{0:T(128)S(1)} %broadcast_add_fusion, s32[48]{0:T(128)S(1)} %copy-done.3), kind=kOutput, calls=%fused_computation.11 | convolution fusion | flops 80464896 | bytes 1450432 | tf_op jit(solution)/shard_map/dot_general | solution.py:60
  (21 shorter events, 9.0 us)
Async XLA Ops:
  0.0 3.6 %copy-start = (bf16[768,2304]{1,0:T(8,128)(2,1)S(1)}, bf16[768,2304]{1,0:T(8,128)(2,1)}, u32[]{:S(2)}) copy-start(bf16[768,2304]{1,0:T(8,128)(2,1)} %param.6) | copy-start | bytes 10616836
  3.0 14.6 %copy-start.2 = (s32[24,2]{0,1:T(2,128)S(1)}, s32[24,2]{0,1:T(2,128)}, u32[]{:S(2)}) copy-start(s32[24,2]{0,1:T(2,128)} %param.8) | copy-start | bytes 580
  10.3 15.7 %all-to-all-start = ((bf16[8,3,2,1,2304]{4,2,1,3,0:T(2,128)(2,1)}), bf16[8,3,2,1,2304]{4,2,1,3,0:T(2,128)(2,1)}, u32[]{:S(2)}, u32[]{:S(2)}) async-start(bf16[8,3,2,1,2304]{4,2,1,3,0:T(2,128)(2,1)} %bitcast.36), calls=%async_computation | async-start | bytes 442368 | tf_op jit(solution)/shard_map/all_to_all | solution.py:42
  30.5 37.6 %copy-start.3 = (s32[48]{0:T(128)S(1)}, s32[48]{0:T(128)}, u32[]{:S(2)}) copy-start(s32[48]{0:T(128)} %eq.28) | copy-start | bytes 580
  40.2 0.7 %copy-start.1 = (f32[6,12,8,16]{3,2,1,0:T(8,128)}, f32[6,12,8,16]{3,2,1,0:T(8,128)S(1)}, u32[]{:S(2)}) copy-start(f32[6,12,8,16]{3,2,1,0:T(8,128)S(1)} %convolution_multiply_fusion) | copy-start | bytes 110596
  55.6 11.0 %all-to-all-start.1 = ((bf16[1,3,2,8,768]{4,2,1,0,3:T(2,128)(2,1)}), bf16[1,3,2,8,768]{4,2,1,0,3:T(2,128)(2,1)}, u32[]{:S(2)}, u32[]{:S(2)}) async-start(bf16[1,3,2,8,768]{4,2,1,0,3:T(2,128)(2,1)} %copy.52), calls=%async_computation.1 | async-start | bytes 147456 | tf_op jit(solution)/shard_map/all_to_all | solution.py:46
where the time goes:
time: 72 us; the launch traced here: 70.6 us
  local copies, waits for them, and re-layouts  31.7 us (44%)
  starting transfers between devices  11.2 us (16%)
  waiting for transfers between devices  10.6 us (15%)
  matrix products  9.2 us (13%)
  other arithmetic  5.8 us (8%)
  blocking collectives  2 us (3%)
    all_to_all x1, starting transfers between devices, local(): lax.all_to_all(outgoing, 'pairs', split_axis=0, concat_axis=3, tiled=True)  7.25 us
    all_to_all x1, waiting for transfers between devices, local(): lax.all_to_all(message, 'pairs', split_axis=3, concat_axis=0, tiled=True)  6.97 us
    gather x2, local copies, waits for them, and re-layouts, local(): outgoing = projected[table_ends]  4.29 us
    all_to_all x1, starting transfers between devices, local(): lax.all_to_all(message, 'pairs', split_axis=3, concat_axis=0, tiled=True)  3.98 us
    rev x1, local copies, waits for them, and re-layouts, cross_both(): split_k = key_rows[:, ::-1].reshape(batch, key_len, HEADS, HDIM)  3.74 us
    rev x1, local copies, waits for them, and re-layouts, cross_both(): split_v = value_rows[:, ::-1].reshape(batch, key_len, HEADS, HDIM)  3.71 us
    all_to_all x1, waiting for transfers between devices, local(): lax.all_to_all(outgoing, 'pairs', split_axis=0, concat_axis=3, tiled=True)  3.65 us
    dot_general x1, matrix products, cross_both(): jnp.einsum('nhqs,nshc->nqhc', softmax, split_v, preferred_element_type=jn...  2.99 us
  transfers between devices with their start and end apart: 2, of which 2 were waited for; matrix products, arithmetic and copies ran while one was open for 7% of the time, Pallas kernels for 0%

commit v1 on v0

v1 whole, which is shorter than its diff:
```python
import functools

import jax
import jax.numpy as jnp
from jax import lax
from jax.experimental import pallas as pl
from jax.experimental.pallas import tpu as pltpu
from jax.sharding import PartitionSpec as P

HDIM = 64
LANES = 128
ROWS = 16
F32 = jnp.float32
BF16 = jnp.bfloat16


def iota(shape, axis):
    return lax.broadcasted_iota(jnp.int32, shape, axis)


def onehot(mask):
    return jnp.where(mask, 1.0, 0.0).astype(BF16)


def dot(a, b):
    return jnp.dot(a, b, preferred_element_type=F32)


def each_chunk(count, body):
    if count == 1:
        body(0)
    else:
        lax.fori_loop(0, count, lambda i, c: (body(i), c)[1], 0)


def rows_at(start, size):
    if isinstance(start, int):
        return pl.ds(start, size)
    return pl.ds(pl.multiple_of(start, ROWS), size)


def kernel(
    n, row_devices, img_hbm, wq_hbm, wo_hbm, ends_ref, weight_ref, out_ref,
    img, wq, wo, send, recv, send2, recv2, proj, stack, combine,
    load_sem, send_sem, recv_sem,
):
    imgs, d = img.shape
    slots = ends_ref.shape[1]
    col_blocks = d // LANES
    chunks = n // ROWS
    block = ROWS * ROWS
    pairs_pos = lax.axis_index("pairs")
    rows_pos = lax.axis_index("rows")
    me = pairs_pos * row_devices + rows_pos

    loads = [
        pltpu.make_async_copy(src, dst, load_sem.at[i])
        for i, (src, dst) in enumerate([(img_hbm, img), (wq_hbm, wq), (wo_hbm, wo)])
    ]
    for load in loads:
        load.start()

    def partner(step):
        other = lax.rem(me + step, n)
        return other, {"pairs": other // row_devices, "rows": lax.rem(other, row_devices)}

    barrier = pltpu.get_barrier_semaphore()

    def greet(step, carry):
        pl.semaphore_signal(
            barrier, inc=1, device_id=partner(step)[1], device_id_type=pl.DeviceIdType.MESH
        )
        return carry

    lax.fori_loop(1, n, greet, 0)

    sub = iota((slots, slots), 0)
    lane = iota((slots, slots), 1)
    w_row = weight_ref[...].astype(F32)
    w_col = jnp.sum(jnp.where(sub == lane, w_row, 0.0), axis=1, keepdims=True)
    ends = ends_ref[...].astype(F32)
    end_row = [ends[e:e + 1] for e in range(2)]
    end_col = [
        jnp.sum(jnp.where(sub == lane, row, 0.0), axis=1, keepdims=True) for row in end_row
    ]
    live_row = jnp.where(w_row > 0, 1.0, 0.0)
    live_col = jnp.where(w_col > 0, 1.0, 0.0)
    rank_row = jnp.sum(jnp.where(sub < lane, live_col, 0.0), axis=0, keepdims=True)
    rank_col = jnp.sum(jnp.where(lane < sub, live_row, 0.0), axis=1, keepdims=True)
    rank_row = jnp.where(w_row > 0, rank_row, -1.0)
    rank_col = jnp.where(w_col > 0, rank_col, -1.0)

    loads[0].wait()
    image_stack = jnp.concatenate(
        [img[:, c * LANES:(c + 1) * LANES] for c in range(col_blocks)], axis=0
    )
    per_tile = LANES // imgs

    def fill(ch):
        row = iota((block, 1), 0)
        place = (row // ROWS + ch * ROWS).astype(F32)
        kind = row % ROWS
        chosen = jnp.where(kind >= col_blocks, end_row[1], end_row[0])
        image = jnp.sum(jnp.where(rank_row == place, chosen, 0.0), axis=1, keepdims=True)
        column = jnp.where(kind >= col_blocks, kind - col_blocks, kind)
        column = jnp.where(kind >= 2 * col_blocks, -1, column)
        across = iota((1, LANES), 1)
        which = (across % imgs).astype(F32)
        parts = [
            onehot((image == which) & (column == m * per_tile + across // imgs))
            for m in range(col_blocks // per_tile)
        ]
        picked = dot(jnp.concatenate(parts, axis=1), image_stack)
        send[rows_at(ch * block, block), :] = picked.astype(BF16)

    each_chunk(chunks, fill)

    pl.semaphore_wait(barrier, n - 1)

    def exchange(source, target, which):
        def one(step, carry):
            other, where = partner(step)
            pltpu.make_async_remote_copy(
                src_ref=source.at[rows_at(other * ROWS, ROWS)],
                dst_ref=target.at[rows_at(me * ROWS, ROWS)],
                send_sem=send_sem.at[which],
                recv_sem=recv_sem.at[which],
                device_id=where,
                device_id_type=pl.DeviceIdType.MESH,
            ).start()
            return carry

        lax.fori_loop(1, n, one, 0)
        target[rows_at(me * ROWS, ROWS), :] = source[rows_at(me * ROWS, ROWS), :]

    def await_all(buffer, sem):
        whole = buffer.at[pl.ds(0, (n - 1) * ROWS)]
        pltpu.make_async_copy(whole, whole, sem).wait()

    exchange(send, recv, 0)

    def fill_combine(ch):
        across = iota((1, block), 1)
        place = (across // ROWS + ch * ROWS).astype(F32)
        kind = across % ROWS
        chosen = jnp.where(kind >= col_blocks, end_col[1], end_col[0])
        image = jnp.sum(jnp.where(rank_col == place, chosen, 0.0), axis=0, keepdims=True)
        column = jnp.where(kind >= col_blocks, kind - col_blocks, kind)
        column = jnp.where(kind >= 2 * col_blocks, -1, column)
        same = image == iota((imgs, 1), 0).astype(F32)
        for c in range(col_blocks):
            combine[ch, c * imgs:(c + 1) * imgs, :] = onehot(same & (column == c))

    each_chunk(chunks, fill_combine)
    number = iota((imgs, 1), 0).astype(F32)
    totals = 1.0 + jnp.sum(
        jnp.where(end_row[0] == number, w_row, 0.0) + jnp.where(end_row[1] == number, w_row, 0.0),
        axis=1, keepdims=True,
    )
    my_weight = jnp.sum(
        jnp.where(rank_row == me.astype(F32), w_row, 0.0), axis=1, keepdims=True
    )
    height = 2 * ROWS * col_blocks

    def spot(row):
        return (row % ROWS) * ROWS + (row // ROWS % 2) * col_blocks + row // (2 * ROWS)

    unpack = onehot(spot(iota((height, 1), 0)) == iota((1, block), 1))
    pack = onehot(spot(iota((1, height), 1)) == iota((block, 1), 0))
    head_of = iota((1, 4 * HDIM), 1) // HDIM
    heads = [onehot(head_of == h) for h in range(4)]
    heads32 = [jnp.where(head_of == h, 1.0, 0.0) for h in range(4)]

    await_all(recv, recv_sem.at[0])
    loads[1].wait()

    def project(ch):
        tokens = dot(unpack, recv[rows_at(ch * block, block), :]).astype(BF16)
        tokens = jnp.concatenate(
            [tokens[c * 2 * ROWS:(c + 1) * 2 * ROWS] for c in range(col_blocks)], axis=1
        )
        for part in range(3):
            result = dot(tokens, wq[:, part * d:(part + 1) * d]).astype(BF16)
            for e in range(2):
                proj[rows_at(e * n + ch * ROWS, ROWS), part * d:(part + 1) * d] = (
                    result[e * ROWS:(e + 1) * ROWS]
                )

    each_chunk(chunks, project)

    def attend(ch):
        for e in range(2):
            for b in range(d // (4 * HDIM)):
                lo = b * 4 * HDIM
                hi = lo + 4 * HDIM
                query = proj[rows_at(e * n + ch * ROWS, ROWS), lo:hi]
                keys = proj[(1 - e) * n:(2 - e) * n, d + lo:d + hi]
                values = proj[(1 - e) * n:(2 - e) * n, 2 * d + lo:2 * d + hi]
                split = jnp.concatenate([query * mask for mask in heads], axis=0)
                scores = lax.dot_general(
                    split, keys, (((1,), (1,)), ((), ())), preferred_element_type=F32
                ) * HDIM ** (-0.5)
                largest = jnp.max(scores, axis=1, keepdims=True)
                exponent = jnp.exp(scores - largest)
                softmax = (exponent / jnp.sum(exponent, axis=1, keepdims=True)).astype(BF16)
                blended = dot(softmax, values)
                attended = sum(
                    blended[h * ROWS:(h + 1) * ROWS] * heads32[h] for h in range(4)
                )
                message = (attended * my_weight).astype(BF16)
                for half in range(2):
                    c = 2 * b + half
                    stack[c * 2 * ROWS + e * ROWS:c * 2 * ROWS + (e + 1) * ROWS, :] = (
                        message[:, half * LANES:(half + 1) * LANES]
                    )
        send2[rows_at(ch * block, block), :] = dot(pack, stack[...]).astype(BF16)

    each_chunk(chunks, attend)

    exchange(send2, recv2, 1)
    loads[2].wait()
    await_all(send, send_sem.at[0])
    await_all(recv2, recv_sem.at[1])

    def add_up(ch):
        return dot(combine[ch], recv2[rows_at(ch * block, block), :])

    if chunks == 1:
        summed = add_up(0)
    else:
        summed = lax.fori_loop(
            1, chunks, lambda ch, total: total + add_up(ch), add_up(0)
        )
    average = jnp.concatenate(
        [(summed[c * imgs:(c + 1) * imgs] / totals).astype(BF16) for c in range(col_blocks)],
        axis=1,
    )
    update = dot(average, wo[...])
    out_ref[...] = (img[...].astype(F32) + update).astype(BF16)
    await_all(send2, send_sem.at[1])


def local(images, w_qkv, w_out, pair_list, pair_weight):
    row_devices = lax.axis_size("rows")
    n = lax.axis_size("pairs") * row_devices
    imgs, local_tokens, d = images.shape
    assert local_tokens == 1 and n % ROWS == 0
    slots = pair_list.shape[0]
    any_space = pl.BlockSpec(memory_space=pl.ANY)
    vmem = pl.BlockSpec(memory_space=pltpu.VMEM)
    col_blocks = d // LANES
    buffer = pltpu.VMEM((n * ROWS, LANES), BF16)
    flat = images.reshape(imgs, d)
    result = pl.pallas_call(
        functools.partial(kernel, n, row_devices),
        out_shape=jax.ShapeDtypeStruct((imgs, d), BF16),
        in_specs=[any_space, any_space, any_space, vmem, vmem],
        out_specs=vmem,
        scratch_shapes=[
            pltpu.VMEM((imgs, d), BF16),
            pltpu.VMEM(w_qkv.shape, BF16),
            pltpu.VMEM(w_out.shape, BF16),
            buffer, buffer, buffer, buffer,
            pltpu.VMEM((2 * n, 3 * d), BF16),
            pltpu.VMEM((2 * ROWS * col_blocks, LANES), BF16),
            pltpu.VMEM((n // ROWS, imgs * col_blocks, ROWS * ROWS), BF16),
            pltpu.SemaphoreType.DMA((3,)),
            pltpu.SemaphoreType.DMA((2,)),
            pltpu.SemaphoreType.DMA((2,)),
        ],
        compiler_params=pltpu.CompilerParams(
            collective_id=0, has_side_effects=True, vmem_limit_bytes=56 * 1024 * 1024
        ),
    )(flat, w_qkv, w_out, pair_list.T, pair_weight.reshape(1, slots))
    return result.reshape(images.shape)


def solution(mesh):
    in_specs = (P("groups", ("pairs", "rows"), None), P(), P(), P("groups", None), P("groups"))
    out_specs = P("groups", ("pairs", "rows"), None)
    return jax.shard_map(local, mesh=mesh, in_specs=in_specs, out_specs=out_specs, check_vma=False)
```

time: 72 us -> 20 us (0.28); the launches traced: 70.6 us -> 19.8 us
  local copies, waits for them, and re-layouts: 31.7 us -> 1.54 us
  Pallas kernels: 0 us -> 18.3 us
  starting transfers between devices: 11.2 us -> 0 us
  waiting for transfers between devices: 10.6 us -> 0 us
  matrix products: 9.2 us -> 0 us
  other arithmetic: 5.8 us -> 0 us
  blocking collectives: 2 us -> 0 us
    pallas_call x0 -> x1, Pallas kernels: none -> 18.3 us  [local(): pl.pallas_call(functools.partial(kernel, n, row_devices), out_shape=jax.S...]
    all_to_all x2 -> x0, starting transfers between devices: 11.2 us -> none  [the longest x1 7.25 us: local(): lax.all_to_all(outgoing, 'pairs', split_axis=0, concat_axis=3, tiled=True)]
    reshape x7 -> x0, local copies, waits for them, and re-layouts: 11.1 us -> none  [the longest x1 1.9 us: cross_both(): split_v = value_rows[:, ::-1].reshape(batch, key_len, HEADS, HDIM)]
    all_to_all x2 -> x0, waiting for transfers between devices: 10.6 us -> none  [the longest x1 6.97 us: local(): lax.all_to_all(message, 'pairs', split_axis=3, concat_axis=0, tiled=True)]
    dot_general x4 -> x0, matrix products: 9.2 us -> none  [the longest x1 2.99 us: cross_both(): jnp.einsum('nhqs,nshc->nqhc', softmax, split_v, preferred_element_type=jn...]
    rev x2 -> x0, local copies, waits for them, and re-layouts: 7.45 us -> none  [the longest x1 3.74 us: cross_both(): split_k = key_rows[:, ::-1].reshape(batch, key_len, HEADS, HDIM)]
    gather x2 -> x0, local copies, waits for them, and re-layouts: 4.29 us -> none  [local(): outgoing = projected[table_ends]]
    slice x3 -> x0, local copies, waits for them, and re-layouts: 3.51 us -> none  [the longest x1 1.57 us: local(): own_half[..., :D]]
  transfers between devices with their start and end apart: 2 -> 0, of which waited for: 2 -> 0; matrix products, arithmetic and copies ran while one was open for 7% -> 0% of each run, Pallas kernels for 0% -> 0%
where the time goes in v1:
time: 20 us; the launch traced here: 19.8 us
  Pallas kernels  18.3 us (92%)
  local copies, waits for them, and re-layouts  1.54 us (8%)
    pallas_call x1, Pallas kernels, local(): pl.pallas_call(functools.partial(kernel, n, row_devices), out_shape=jax.S...  18.3 us
    unnamed x1, local copies, waits for them, and re-layouts  1.54 us

profile of v1, /device:TPU:0, one launch (start us, length us, event | category | flops | bytes accessed | tf_op | source)
XLA Modules:
  0.0 19.8 jit_solution(16743548988989881286)
XLA Ops:
  0.0 18.3 %shard_map.55 = bf16[64,768]{1,0:T(8,128)(2,1)} custom-call(bf16[64,768]{1,0:T(8,128)(2,1)} %bitcast.5, bf16[768,2304]{1,0:T(8,128)(2,1)} %wq_hbm.1, bf16[768,768]{1,0:T(8,128)(2,1)} %wo_hbm.1, s32[2,24]{1,0:T(2,128)} %bitcast.6, s32[1,24]{1,0:T(1,128)} %bitcast.7), custom_call_target="tpu_custom_call" | custom-call | tf_op jit(solution)/shard_map/pallas_call | solution.py:254
  18.3 1.5 %copy.7 = bf16[64,1,768]{2,0,1:T(8,128)(2,1)} copy(bf16[64,1,768]{2,0,1:T(8,128)(2,1)} %bitcast.4) | data formatting | bytes 196608

commit v2 on v1

--- a/solution.py
+++ b/solution.py
@@ -40,8 +40,8 @@
 
 
 def kernel(
-    n, row_devices, img_hbm, wq_hbm, wo_hbm, ends_ref, weight_ref, out_ref,
-    img, wq, wo, send, recv, send2, recv2, proj, stack, combine,
+    n, row_devices, img_hbm, wq_hbm, ends_hbm, weight_hbm, out_ref,
+    ends_ref, weight_ref, img, wq, send, recv, send2, recv2, proj, stack, combine,
     load_sem, send_sem, recv_sem,
 ):
     imgs, d = img.shape
@@ -53,16 +53,28 @@
     rows_pos = lax.axis_index("rows")
     me = pairs_pos * row_devices + rows_pos
 
+    pairs_of_refs = [
+        (ends_hbm, ends_ref), (weight_hbm, weight_ref), (img_hbm, img), (wq_hbm, wq)
+    ]
     loads = [
         pltpu.make_async_copy(src, dst, load_sem.at[i])
-        for i, (src, dst) in enumerate([(img_hbm, img), (wq_hbm, wq), (wo_hbm, wo)])
+        for i, (src, dst) in enumerate(pairs_of_refs)
     ]
-    for load in loads:
-        load.start()
 
     def partner(step):
-        other = lax.rem(me + step, n)
+        other = me
+        bit = 1
+        while bit < n:
+            other = other + (step // bit % 2) * (1 - 2 * (me // bit % 2)) * bit
+            bit *= 2
         return other, {"pairs": other // row_devices, "rows": lax.rem(other, row_devices)}
+
+    def each_partner(body):
+        if chunks == 1:
+            for step in range(n - 1, 0, -1):
+                body(step, 0)
+        else:
+            lax.fori_loop(1, n, lambda i, c: body(n - i, c), 0)
 
     barrier = pltpu.get_barrier_semaphore()
 
@@ -72,7 +84,13 @@
         )
         return carry
 
-    lax.fori_loop(1, n, greet, 0)
+    each_partner(greet)
+
+    for load in loads:
+        load.start()
+
+    loads[0].wait()
+    loads[1].wait()
 
     sub = iota((slots, slots), 0)
     lane = iota((slots, slots), 1)
@@ -90,7 +108,7 @@
     rank_row = jnp.where(w_row > 0, rank_row, -1.0)
     rank_col = jnp.where(w_col > 0, rank_col, -1.0)
 
-    loads[0].wait()
+    loads[2].wait()
     image_stack = jnp.concatenate(
         [img[:, c * LANES:(c + 1) * LANES] for c in range(col_blocks)], axis=0
     )
@@ -130,7 +148,7 @@
             ).start()
             return carry
 
-        lax.fori_loop(1, n, one, 0)
+        each_partner(one)
         target[rows_at(me * ROWS, ROWS), :] = source[rows_at(me * ROWS, ROWS), :]
 
     def await_all(buffer, sem):
@@ -172,7 +190,7 @@
     heads32 = [jnp.where(head_of == h, 1.0, 0.0) for h in range(4)]
 
     await_all(recv, recv_sem.at[0])
-    loads[1].wait()
+    loads[3].wait()
 
     def project(ch):
         tokens = dot(unpack, recv[rows_at(ch * block, block), :]).astype(BF16)
@@ -218,7 +236,6 @@
     each_chunk(chunks, attend)
 
     exchange(send2, recv2, 1)
-    loads[2].wait()
     await_all(send, send_sem.at[0])
     await_all(recv2, recv_sem.at[1])
 
@@ -235,8 +252,7 @@
         [(summed[c * imgs:(c + 1) * imgs] / totals).astype(BF16) for c in range(col_blocks)],
         axis=1,
     )
-    update = dot(average, wo[...])
-    out_ref[...] = (img[...].astype(F32) + update).astype(BF16)
+    out_ref[...] = average
     await_all(send2, send_sem.at[1])
 
 
@@ -253,26 +269,28 @@
     flat = images.reshape(imgs, d)
     result = pl.pallas_call(
         functools.partial(kernel, n, row_devices),
-        out_shape=jax.ShapeDtypeStruct((imgs, d), BF16),
-        in_specs=[any_space, any_space, any_space, vmem, vmem],
+        out_shape=pltpu.VMEM((imgs, d), BF16),
+        in_specs=[any_space] * 4,
         out_specs=vmem,
         scratch_shapes=[
+            pltpu.VMEM((2, slots), jnp.int32),
+            pltpu.VMEM((1, slots), jnp.int32),
             pltpu.VMEM((imgs, d), BF16),
             pltpu.VMEM(w_qkv.shape, BF16),
-            pltpu.VMEM(w_out.shape, BF16),
             buffer, buffer, buffer, buffer,
             pltpu.VMEM((2 * n, 3 * d), BF16),
             pltpu.VMEM((2 * ROWS * col_blocks, LANES), BF16),
             pltpu.VMEM((n // ROWS, imgs * col_blocks, ROWS * ROWS), BF16),
-            pltpu.SemaphoreType.DMA((3,)),
+            pltpu.SemaphoreType.DMA((4,)),
             pltpu.SemaphoreType.DMA((2,)),
             pltpu.SemaphoreType.DMA((2,)),
         ],
         compiler_params=pltpu.CompilerParams(
             collective_id=0, has_side_effects=True, vmem_limit_bytes=56 * 1024 * 1024
         ),
-    )(flat, w_qkv, w_out, pair_list.T, pair_weight.reshape(1, slots))
-    return result.reshape(images.shape)
+    )(flat, w_qkv, pair_list.T, pair_weight.reshape(1, slots))
+    update = jnp.dot(result, w_out, preferred_element_type=F32)
+    return (flat.astype(F32) + update).astype(BF16).reshape(images.shape)
 
 
 def solution(mesh):

time: 20 us -> 17.4 us (0.87)
  Pallas kernels: 18.3 us -> 16.3 us
  local copies, waits for them, and re-layouts: 1.54 us -> 0.01 us
  matrix products: 0 us -> 0.98 us
    pallas_call x1, Pallas kernels: 18.3 us -> 16.3 us  [local(): pl.pallas_call(functools.partial(kernel, n, row_devices), out_shape=pltpu...]
    unnamed x1 -> x4, local copies, waits for them, and re-layouts: 1.54 us -> 0.01 us
    dot_general x0 -> x1, matrix products: none -> 0.98 us  [local(): update = jnp.dot(result, w_out, preferred_element_type=F32)]
where the time goes in v2:
time: 17.4 us; the launch traced here: 17.3 us
  Pallas kernels  16.3 us (94%)
  matrix products  0.98 us (6%)
    pallas_call x1, Pallas kernels, local(): pl.pallas_call(functools.partial(kernel, n, row_devices), out_shape=pltpu...  16.3 us
    dot_general x1, matrix products, local(): update = jnp.dot(result, w_out, preferred_element_type=F32)  0.98 us

profile of v2, /device:TPU:0, one launch (start us, length us, event | category | flops | bytes accessed | tf_op | source)
XLA Modules:
  0.0 17.3 jit_solution(17575278696770727935)
XLA Ops:
  0.0 0.0 copy-start
  0.0 0.0 copy-start.1
  0.0 16.3 %shard_map.55 = bf16[64,768]{1,0:T(8,128)(2,1)S(1)} custom-call(bf16[64,768]{1,0:T(8,128)(2,1)} %bitcast.8, bf16[768,2304]{1,0:T(8,128)(2,1)} %wq_hbm.1, s32[2,24]{1,0:T(2,128)} %bitcast.9, s32[1,24]{1,0:T(1,128)} %bitcast.10), custom_call_target="tpu_custom_call" | custom-call | tf_op jit(solution)/shard_map/pallas_call | solution.py:270
  16.3 0.0 copy-done
  16.3 0.0 copy-done.1
  16.3 1.0 %fusion.1 = bf16[64,1,768]{2,0,1:T(8,128)(2,1)} fusion(bf16[64,768]{1,0:T(8,128)(2,1)S(1)} %shard_map.55, bf16[768,768]{1,0:T(8,128)(2,1)S(1)} %copy-done, bf16[64,1,768]{2,0,1:T(8,128)(2,1)S(1)} %copy-done.1), kind=kOutput, calls=%fused_computation.2 | convolution fusion | flops 75644928 | bytes 1474560 | tf_op jit(solution)/shard_map/dot_general | solution.py:292
Async XLA Ops:
  0.0 16.3 %copy-start = (bf16[768,768]{1,0:T(8,128)(2,1)S(1)}, bf16[768,768]{1,0:T(8,128)(2,1)}, u32[]{:S(2)}) copy-start(bf16[768,768]{1,0:T(8,128)(2,1)} %param.7) | copy-start | bytes 3538948
  0.0 16.3 %copy-start.1 = (bf16[64,1,768]{2,0,1:T(8,128)(2,1)S(1)}, bf16[64,1,768]{2,0,1:T(8,128)(2,1)}, u32[]{:S(2)}) copy-start(bf16[64,1,768]{2,0,1:T(8,128)(2,1)} %param.5) | copy-start | bytes 294916

commit v3 on v2

--- a/solution.py
+++ b/solution.py
@@ -78,10 +78,23 @@
 
     barrier = pltpu.get_barrier_semaphore()
 
+    workers = n // 2
+    first = n // 4
+
+    def works(device):
+        return (device >= first) & (device < first + workers)
+
+    i_work = works(me)
+
     def greet(step, carry):
-        pl.semaphore_signal(
-            barrier, inc=1, device_id=partner(step)[1], device_id_type=pl.DeviceIdType.MESH
-        )
+        other, where = partner(step)
+
+        @pl.when(i_work | works(other))
+        def _():
+            pl.semaphore_signal(
+                barrier, inc=1, device_id=where, device_id_type=pl.DeviceIdType.MESH
+            )
+
         return carry
 
     each_partner(greet)
@@ -133,29 +146,51 @@
 
     each_chunk(chunks, fill)
 
-    pl.semaphore_wait(barrier, n - 1)
-
-    def exchange(source, target, which):
-        def one(step, carry):
-            other, where = partner(step)
-            pltpu.make_async_remote_copy(
-                src_ref=source.at[rows_at(other * ROWS, ROWS)],
-                dst_ref=target.at[rows_at(me * ROWS, ROWS)],
-                send_sem=send_sem.at[which],
-                recv_sem=recv_sem.at[which],
-                device_id=where,
-                device_id_type=pl.DeviceIdType.MESH,
-            ).start()
-            return carry
-
-        each_partner(one)
-        target[rows_at(me * ROWS, ROWS), :] = source[rows_at(me * ROWS, ROWS), :]
-
-    def await_all(buffer, sem):
-        whole = buffer.at[pl.ds(0, (n - 1) * ROWS)]
+    @pl.when(i_work)
+    def _():
+        pl.semaphore_wait(barrier, n - 1)
+
+    @pl.when(jnp.logical_not(i_work))
+    def _():
+        pl.semaphore_wait(barrier, workers)
+
+    def move(source, target, where, which):
+        pltpu.make_async_remote_copy(
+            src_ref=source,
+            dst_ref=target,
+            send_sem=send_sem.at[which],
+            recv_sem=recv_sem.at[which],
+            device_id=where,
+            device_id_type=pl.DeviceIdType.MESH,
+        ).start()
+
+    def await_blocks(blocks, sem):
+        whole = recv.at[pl.ds(0, blocks * ROWS)]
         pltpu.make_async_copy(whole, whole, sem).wait()
 
-    exchange(send, recv, 0)
+    def send_tokens(step, carry):
+        other, where = partner(step)
+
+        @pl.when(works(other))
+        def _():
+            for q in range(2):
+                move(
+                    send.at[rows_at((2 * (other - first) + q) * ROWS, ROWS)],
+                    recv.at[rows_at(q * n * ROWS + me * ROWS, ROWS)], where, 0,
+                )
+
+        return carry
+
+    def send_messages(step, carry):
+        other, where = partner(step)
+        for q in range(2):
+            move(
+                send2.at[rows_at(q * n * ROWS + other * ROWS, ROWS)],
+                recv2.at[rows_at((2 * (me - first) + q) * ROWS, ROWS)], where, 1,
+            )
+        return carry
+
+    each_partner(send_tokens)
 
     def fill_combine(ch):
         across = iota((1, block), 1)
@@ -175,9 +210,13 @@
         jnp.where(end_row[0] == number, w_row, 0.0) + jnp.where(end_row[1] == number, w_row, 0.0),
         axis=1, keepdims=True,
     )
-    my_weight = jnp.sum(
-        jnp.where(rank_row == me.astype(F32), w_row, 0.0), axis=1, keepdims=True
-    )
+    my_weight = [
+        jnp.sum(
+            jnp.where(rank_row == (2 * (me - first) + q).astype(F32), w_row, 0.0),
+            axis=1, keepdims=True,
+        )
+        for q in range(2)
+    ]
     height = 2 * ROWS * col_blocks
 
     def spot(row):
@@ -189,55 +228,81 @@
     heads = [onehot(head_of == h) for h in range(4)]
     heads32 = [jnp.where(head_of == h, 1.0, 0.0) for h in range(4)]
 
-    await_all(recv, recv_sem.at[0])
     loads[3].wait()
 
-    def project(ch):
-        tokens = dot(unpack, recv[rows_at(ch * block, block), :]).astype(BF16)
-        tokens = jnp.concatenate(
-            [tokens[c * 2 * ROWS:(c + 1) * 2 * ROWS] for c in range(col_blocks)], axis=1
-        )
-        for part in range(3):
-            result = dot(tokens, wq[:, part * d:(part + 1) * d]).astype(BF16)
-            for e in range(2):
-                proj[rows_at(e * n + ch * ROWS, ROWS), part * d:(part + 1) * d] = (
-                    result[e * ROWS:(e + 1) * ROWS]
-                )
-
-    each_chunk(chunks, project)
-
-    def attend(ch):
-        for e in range(2):
+    @pl.when(i_work)
+    def _():
+        for q in range(2):
+            recv[rows_at(q * n * ROWS + me * ROWS, ROWS), :] = (
+                send[rows_at((2 * (me - first) + q) * ROWS, ROWS), :]
+            )
+        await_blocks(2 * (n - 1), recv_sem.at[0])
+
+        def project(ch):
+            both = []
+            for q in range(2):
+                tokens = dot(unpack, recv[rows_at(q * n * ROWS + ch * block, block), :]).astype(BF16)
+                both.append(jnp.concatenate(
+                    [tokens[c * 2 * ROWS:(c + 1) * 2 * ROWS] for c in range(col_blocks)], axis=1
+                ))
+            tokens = jnp.concatenate(both, axis=0)
+            for part in range(3):
+                result = dot(tokens, wq[:, part * d:(part + 1) * d]).astype(BF16)
+                for e in range(4):
+                    proj[rows_at(e * n + ch * ROWS, ROWS), part * d:(part + 1) * d] = (
+                        result[e * ROWS:(e + 1) * ROWS]
+                    )
+
+        each_chunk(chunks, project)
+
+        group = iota((16 * ROWS, 1), 0) // ROWS % 4
+        allowed = group + 1 - 2 * (group % 2) == iota((1, 4 * n), 1) // n
+
+        def attend(ch):
             for b in range(d // (4 * HDIM)):
                 lo = b * 4 * HDIM
                 hi = lo + 4 * HDIM
-                query = proj[rows_at(e * n + ch * ROWS, ROWS), lo:hi]
-                keys = proj[(1 - e) * n:(2 - e) * n, d + lo:d + hi]
-                values = proj[(1 - e) * n:(2 - e) * n, 2 * d + lo:2 * d + hi]
+                query = jnp.concatenate(
+                    [proj[rows_at(own * n + ch * ROWS, ROWS), lo:hi] for own in range(4)], axis=0
+                )
                 split = jnp.concatenate([query * mask for mask in heads], axis=0)
                 scores = lax.dot_general(
-                    split, keys, (((1,), (1,)), ((), ())), preferred_element_type=F32
+                    split, proj[:, d + lo:d + hi], (((1,), (1,)), ((), ())),
+                    preferred_element_type=F32,
                 ) * HDIM ** (-0.5)
+                scores = jnp.where(allowed, scores, -jnp.inf)
                 largest = jnp.max(scores, axis=1, keepdims=True)
                 exponent = jnp.exp(scores - largest)
-                softmax = (exponent / jnp.sum(exponent, axis=1, keepdims=True)).astype(BF16)
-                blended = dot(softmax, values)
-                attended = sum(
-                    blended[h * ROWS:(h + 1) * ROWS] * heads32[h] for h in range(4)
-                )
-                message = (attended * my_weight).astype(BF16)
-                for half in range(2):
-                    c = 2 * b + half
-                    stack[c * 2 * ROWS + e * ROWS:c * 2 * ROWS + (e + 1) * ROWS, :] = (
-                        message[:, half * LANES:(half + 1) * LANES]
+                total = jnp.sum(exponent, axis=1, keepdims=True)
+                softmax = (exponent / total).astype(BF16)
+                blended = dot(softmax, proj[:, 2 * d + lo:2 * d + hi])
+                for own in range(4):
+                    attended = sum(
+                        blended[(4 * h + own) * ROWS:(4 * h + own + 1) * ROWS] * heads32[h]
+                        for h in range(4)
                     )
-        send2[rows_at(ch * block, block), :] = dot(pack, stack[...]).astype(BF16)
-
-    each_chunk(chunks, attend)
-
-    exchange(send2, recv2, 1)
-    await_all(send, send_sem.at[0])
-    await_all(recv2, recv_sem.at[1])
+                    message = (attended * my_weight[own // 2]).astype(BF16)
+                    for half in range(2):
+                        row = (own // 2) * height + ((2 * b + half) * 2 + own % 2) * ROWS
+                        stack[row:row + ROWS, :] = message[:, half * LANES:(half + 1) * LANES]
+            for q in range(2):
+                send2[rows_at(q * n * ROWS + ch * block, block), :] = dot(
+                    pack, stack[q * height:(q + 1) * height]
+                ).astype(BF16)
+
+        each_chunk(chunks, attend)
+        each_partner(send_messages)
+        for q in range(2):
+            recv2[rows_at((2 * (me - first) + q) * ROWS, ROWS), :] = (
+                send2[rows_at(q * n * ROWS + me * ROWS, ROWS), :]
+            )
+        await_blocks(2 * (workers - 1), send_sem.at[0])
+        await_blocks(2 * (workers - 1), recv_sem.at[1])
+
+    @pl.when(jnp.logical_not(i_work))
+    def _():
+        await_blocks(2 * workers, send_sem.at[0])
+        await_blocks(2 * workers, recv_sem.at[1])
 
     def add_up(ch):
         return dot(combine[ch], recv2[rows_at(ch * block, block), :])
@@ -253,7 +318,10 @@
         axis=1,
     )
     out_ref[...] = average
-    await_all(send2, send_sem.at[1])
+
+    @pl.when(i_work)
+    def _():
+        await_blocks(2 * (n - 1), send_sem.at[1])
 
 
 def local(images, w_qkv, w_out, pair_list, pair_weight):
@@ -266,6 +334,7 @@
     vmem = pl.BlockSpec(memory_space=pltpu.VMEM)
     col_blocks = d // LANES
     buffer = pltpu.VMEM((n * ROWS, LANES), BF16)
+    twice = pltpu.VMEM((2 * n * ROWS, LANES), BF16)
     flat = images.reshape(imgs, d)
     result = pl.pallas_call(
         functools.partial(kernel, n, row_devices),
@@ -277,9 +346,9 @@
             pltpu.VMEM((1, slots), jnp.int32),
             pltpu.VMEM((imgs, d), BF16),
             pltpu.VMEM(w_qkv.shape, BF16),
-            buffer, buffer, buffer, buffer,
-            pltpu.VMEM((2 * n, 3 * d), BF16),
-            pltpu.VMEM((2 * ROWS * col_blocks, LANES), BF16),
+            buffer, twice, twice, buffer,
+            pltpu.VMEM((4 * n, 3 * d), BF16),
+            pltpu.VMEM((4 * ROWS * col_blocks, LANES), BF16),
             pltpu.VMEM((n // ROWS, imgs * col_blocks, ROWS * ROWS), BF16),
             pltpu.SemaphoreType.DMA((4,)),
             pltpu.SemaphoreType.DMA((2,)),

time: 17.4 us -> 16.3 us (0.937)
  Pallas kernels: 16.3 us -> 15.2 us
    pallas_call x1, Pallas kernels: 16.3 us -> 15.2 us  [local(): pl.pallas_call(functools.partial(kernel, n, row_devices), out_shape=pltpu...]
where the time goes in v3:
time: 16.3 us; the launch traced here: 16.2 us
  Pallas kernels  15.2 us (93%)
  matrix products  0.98 us (6%)
    pallas_call x1, Pallas kernels, local(): pl.pallas_call(functools.partial(kernel, n, row_devices), out_shape=pltpu...  15.2 us
    dot_general x1, matrix products, local(): update = jnp.dot(result, w_out, preferred_element_type=F32)  0.98 us

profile of v3, /device:TPU:0, one launch (start us, length us, event | category | flops | bytes accessed | tf_op | source)
XLA Modules:
  0.0 16.2 jit_solution(4434134795326491419)
XLA Ops:
  0.0 0.0 copy-start
  0.0 0.0 copy-start.1
  0.0 15.2 %shard_map.55 = bf16[64,768]{1,0:T(8,128)(2,1)S(1)} custom-call(bf16[64,768]{1,0:T(8,128)(2,1)} %bitcast.8, bf16[768,2304]{1,0:T(8,128)(2,1)} %wq_hbm.1, s32[2,24]{1,0:T(2,128)} %bitcast.9, s32[1,24]{1,0:T(1,128)} %bitcast.10), custom_call_target="tpu_custom_call" | custom-call | tf_op jit(solution)/shard_map/pallas_call | solution.py:339
  15.2 0.0 copy-done
  15.2 0.0 copy-done.1
  15.2 1.0 %fusion.1 = bf16[64,1,768]{2,0,1:T(8,128)(2,1)} fusion(bf16[64,768]{1,0:T(8,128)(2,1)S(1)} %shard_map.55, bf16[768,768]{1,0:T(8,128)(2,1)S(1)} %copy-done, bf16[64,1,768]{2,0,1:T(8,128)(2,1)S(1)} %copy-done.1), kind=kOutput, calls=%fused_computation.2 | convolution fusion | flops 75644928 | bytes 1474560 | tf_op jit(solution)/shard_map/dot_general | solution.py:361
Async XLA Ops:
  0.0 15.2 %copy-start = (bf16[768,768]{1,0:T(8,128)(2,1)S(1)}, bf16[768,768]{1,0:T(8,128)(2,1)}, u32[]{:S(2)}) copy-start(bf16[768,768]{1,0:T(8,128)(2,1)} %param.7) | copy-start | bytes 3538948
  0.0 15.2 %copy-start.1 = (bf16[64,1,768]{2,0,1:T(8,128)(2,1)S(1)}, bf16[64,1,768]{2,0,1:T(8,128)(2,1)}, u32[]{:S(2)}) copy-start(bf16[64,1,768]{2,0,1:T(8,128)(2,1)} %param.5) | copy-start | bytes 294916

commit v4 on v3

--- a/solution.py
+++ b/solution.py
@@ -99,8 +99,12 @@
 
     each_partner(greet)
 
-    for load in loads:
+    for load in loads[:3]:
         load.start()
+
+    @pl.when(i_work)
+    def _():
+        loads[3].start()
 
     loads[0].wait()
     loads[1].wait()
@@ -228,10 +232,9 @@
     heads = [onehot(head_of == h) for h in range(4)]
     heads32 = [jnp.where(head_of == h, 1.0, 0.0) for h in range(4)]
 
-    loads[3].wait()
-
     @pl.when(i_work)
     def _():
+        loads[3].wait()
         for q in range(2):
             recv[rows_at(q * n * ROWS + me * ROWS, ROWS), :] = (
                 send[rows_at((2 * (me - first) + q) * ROWS, ROWS), :]

time: 16.3 us -> 16.3 us (level)
  no operation moved by 1% of the time
where the time goes in v4:
time: 16.3 us; the launch traced here: 16.2 us
  Pallas kernels  15.2 us (93%)
  matrix products  0.98 us (6%)
    pallas_call x1, Pallas kernels, local(): pl.pallas_call(functools.partial(kernel, n, row_devices), out_shape=pltpu...  15.2 us
    dot_general x1, matrix products, local(): update = jnp.dot(result, w_out, preferred_element_type=F32)  0.98 us

profile of v4, /device:TPU:0, one launch (start us, length us, event | category | flops | bytes accessed | tf_op | source)
XLA Modules:
  0.0 16.2 jit_solution(3327729444384709037)
XLA Ops:
  0.0 0.0 copy-start
  0.0 0.0 copy-start.1
  0.0 15.2 %shard_map.55 = bf16[64,768]{1,0:T(8,128)(2,1)S(1)} custom-call(bf16[64,768]{1,0:T(8,128)(2,1)} %bitcast.8, bf16[768,2304]{1,0:T(8,128)(2,1)} %wq_hbm.1, s32[2,24]{1,0:T(2,128)} %bitcast.9, s32[1,24]{1,0:T(1,128)} %bitcast.10), custom_call_target="tpu_custom_call" | custom-call | tf_op jit(solution)/shard_map/pallas_call | solution.py:342
  15.2 0.0 copy-done
  15.2 0.0 copy-done.1
  15.2 1.0 %fusion.1 = bf16[64,1,768]{2,0,1:T(8,128)(2,1)} fusion(bf16[64,768]{1,0:T(8,128)(2,1)S(1)} %shard_map.55, bf16[768,768]{1,0:T(8,128)(2,1)S(1)} %copy-done, bf16[64,1,768]{2,0,1:T(8,128)(2,1)S(1)} %copy-done.1), kind=kOutput, calls=%fused_computation.2 | convolution fusion | flops 75644928 | bytes 1474560 | tf_op jit(solution)/shard_map/dot_general | solution.py:364
Async XLA Ops:
  0.0 15.2 %copy-start = (bf16[768,768]{1,0:T(8,128)(2,1)S(1)}, bf16[768,768]{1,0:T(8,128)(2,1)}, u32[]{:S(2)}) copy-start(bf16[768,768]{1,0:T(8,128)(2,1)} %param.7) | copy-start | bytes 3538948
  0.0 15.2 %copy-start.1 = (bf16[64,1,768]{2,0,1:T(8,128)(2,1)S(1)}, bf16[64,1,768]{2,0,1:T(8,128)(2,1)}, u32[]{:S(2)}) copy-start(bf16[64,1,768]{2,0,1:T(8,128)(2,1)} %param.5) | copy-start | bytes 294916
